TPU v7x, 512 devices: a whole 4x8x8 slice. The times are simulated.
512 devices in a mesh: blk: 8 (over y), uly: 8 (over x, core), tp: 8 (over z).
Axes of the slice: x: 4, y: 8, z: 8, core: 2. Of those that a mesh axis runs over, the one named last changes fastest.
Arguments:
- queries: bfloat16 [8192, 64, 128], P(('blk', 'uly'), 'tp'), may hold values from -84 to 84
- keys: bfloat16 [8192, 8, 128], P(('blk', 'uly'), 'tp'), may hold values from -12 to 12
- values: bfloat16 [8192, 8, 128], P(('blk', 'uly'), 'tp'), may hold values from -6 to 6
- span_order: int32 [16], replicated, may hold values from 0 to 15, each once
Outputs:
- attended: bfloat16 [8192, 64, 128], P(('blk', 'uly'), 'tp')
Inputs may be any that keep to these rules, and one draw needn't show every extreme that they name: `span_order`: holds every number from 0 to 15 exactly once.
All inputs are finite; a program needn't handle non-finite values.
Results may differ from a plain program's by a relative error of at most 0.0065.
Values may be sent and summed in bfloat16 or wider, within the bound.
No kernel may reach another device: no remote copies, remote signals or barrier semaphores. Data moves between devices by JAX's collectives and lax.ppermute only.
A program may use at most 64 MiB of HBM per device.

v0:
```python
import math
import jax
import jax.numpy as jnp
from jax import lax
from jax.sharding import PartitionSpec as P


def span_positions(row_index, span_order, span_len):
    span_index = row_index // span_len
    span_ids = jnp.arange(span_order.shape[0], dtype=jnp.int32)
    span_hit = span_index[:, None] == span_ids[None, :]
    start_pos = jnp.sum(jnp.where(span_hit, span_order[None, :], 0), axis=1)
    return start_pos * span_len + row_index % span_len


def attend_block(carry_state, query_four, query_pos, key_block, value_block, key_pos, score_scale):
    running_max, running_sum, weighted = carry_state
    scores = (
        jnp.einsum("rhgd,phd->rhgp", query_four, key_block, preferred_element_type=jnp.float32)
        * score_scale
    )
    visible = (key_pos[None, :] <= query_pos[:, None])[:, None, None, :]
    scores = jnp.where(visible, scores, -1e30)
    next_max = jnp.maximum(running_max, jnp.max(scores, axis=3))
    weights = jnp.where(visible, jnp.exp(scores - next_max[..., None]), 0.0)
    rescale = jnp.exp(running_max - next_max)
    running_sum = running_sum * rescale + jnp.sum(weights, axis=3)
    weighted = weighted * rescale[..., None] + jnp.einsum(
        "rhgp,phd->rhgd",
        weights.astype(jnp.bfloat16),
        value_block,
        preferred_element_type=jnp.float32,
    )
    return (next_max, running_sum, weighted)


def make_folder(query_four, query_pos, span_order, span_len):
    score_scale = 1.0 / math.sqrt(query_four.shape[3])

    def fold_keys(carry_state, key_piece, start):
        piece_keys, piece_values = key_piece
        piece_rows = piece_keys.shape[0]
        block_rows = 512
        block_count = piece_rows // block_rows
        heads_here = piece_keys.shape[1]
        head_size = piece_keys.shape[2]
        key_blocks = piece_keys.reshape(block_count, block_rows, heads_here, head_size)
        value_blocks = piece_values.reshape(block_count, block_rows, heads_here, head_size)
        key_positions = span_positions(
            jnp.arange(piece_rows, dtype=jnp.int32), span_order, span_len
        )
        key_positions = key_positions.reshape(block_count, block_rows)

        def scan_step(inner_state, block_item):
            key_block, value_block, key_pos = block_item
            inner_state = attend_block(
                inner_state, query_four, query_pos, key_block, value_block, key_pos, score_scale
            )
            return (inner_state, None)

        carry_state, _ = lax.scan(scan_step, carry_state, (key_blocks, value_blocks, key_positions))
        return carry_state

    return fold_keys


def initial_state(query_four):
    lead_shape = query_four.shape[:3]
    return (
        jnp.full(lead_shape, -1e30, jnp.float32),
        jnp.zeros(lead_shape, jnp.float32),
        jnp.zeros(query_four.shape, jnp.float32),
    )


def finish_state(final_state):
    running_max, running_sum, weighted = final_state
    return (weighted / running_sum[..., None]).astype(jnp.bfloat16)


def local(queries, keys, values, span_order):
    tok_rows = queries.shape[0]
    head_size = queries.shape[2]
    uly_size = lax.axis_size("uly")
    span_len = tok_rows * uly_size // 2
    blk_place = lax.axis_index("blk")
    query_heads = lax.all_to_all(queries, "uly", split_axis=1, concat_axis=0, tiled=True)
    local_rows = query_heads.shape[0]
    per_device = query_heads.shape[1]
    query_four = query_heads.reshape(local_rows, 1, per_device, head_size)
    query_pos = span_positions(
        blk_place * local_rows + jnp.arange(local_rows, dtype=jnp.int32), span_order, span_len
    )
    folder = make_folder(query_four, query_pos, span_order, span_len)
    final_state = folder(
        initial_state(query_four),
        (
            lax.all_gather(keys, ("blk", "uly"), axis=0, tiled=True),
            lax.all_gather(values, ("blk", "uly"), axis=0, tiled=True),
        ),
        jnp.int32(0),
    )
    head_output = finish_state(final_state).reshape(local_rows, per_device, head_size)
    return lax.all_to_all(head_output, "uly", split_axis=0, concat_axis=1, tiled=True)


def solution(mesh):
    in_specs = (
        P(("blk", "uly"), "tp", None),
        P(("blk", "uly"), "tp", None),
        P(("blk", "uly"), "tp", None),
        P(),
    )
    out_specs = P(("blk", "uly"), "tp", None)
    return jax.shard_map(local, mesh=mesh, in_specs=in_specs, out_specs=out_specs, check_vma=False)
```

profile of v0, /device:TPU:1, one launch (start us, length us, event | category | flops | bytes accessed | tf_op | source)
XLA Modules:
  0.0 263.5 jit_solution(8121300190383267117)
XLA Ops:
  6.5 0.7 all-gather.3.cloned.1.call-update
  7.3 0.7 all-gather.5.cloned.1.call-update
  8.0 1.7 copy.22
  9.7 10.2 %all-to-all-start = ((bf16[128,8,128]{2,0,1:T(8,128)(2,1)}), bf16[128,8,128]{2,0,1:T(8,128)(2,1)S(1)}, u32[]{:S(2)}, u32[]{:S(2)}) async-start(bf16[128,8,128]{2,0,1:T(8,128)(2,1)} %copy.22), calls=%async_computation | async-start | bytes 524288 | tf_op jit(solution)/shard_map/all_to_all | solution.py:87
  19.9 0.7 select_reduce_fusion.1
  20.7 0.8 select_reduce_fusion
  21.6 4.8 %all-to-all-done = bf16[128,8,128]{2,0,1:T(8,128)(2,1)S(1)} async-done(((bf16[128,8,128]{2,0,1:T(8,128)(2,1)}), bf16[128,8,128]{2,0,1:T(8,128)(2,1)S(1)}, u32[]{:S(2)}, u32[]{:S(2)}) %all-to-all-start) | async-done | bytes 262176 | tf_op jit(solution)/shard_map/all_to_all | solution.py:87
  26.4 72.7 %all-gather.3.cloned.1.call-done = bf16[8192,1,128]{2,0,1:T(8,128)(2,1)} async-done(((bf16[128,1,128]{2,0,1:T(8,128)(2,1)}), bf16[8192,1,128]{2,0,1:T(8,128)(2,1)}) %all-gather.3.cloned.1.call-update) | async-done | bytes 2097168 | tf_op jit(solution)/shard_map/all_gather | solution.py:98
  99.1 83.9 %all-gather.5.cloned.1.call-done = bf16[8192,1,128]{2,0,1:T(8,128)(2,1)} async-done(((bf16[128,1,128]{2,0,1:T(8,128)(2,1)}), bf16[8192,1,128]{2,0,1:T(8,128)(2,1)}) %all-gather.5.cloned.1.call-update) | async-done | bytes 2097168 | tf_op jit(solution)/shard_map/all_gather | solution.py:99
  183.0 60.9 %while.15 = (s32[]{:T(128)}, f32[1024,1,1]{0,2,1:T(1,128)S(1)}, f32[1024,1,1]{0,2,1:T(1,128)S(1)}, f32[1024,1,1,128]{0,3,2,1:T(8,128)S(1)}, s32[16,512]{1,0:T(8,...) while((s32[]{:T(128)}, f32[1024,1,1]{0,2,1:T(1,128)S(1)}, ...), condition=%wide.region_5.6_spmd.clone, body=%wide.region_2.5_spmd.clone.sunk | while | flops 277222400 | bytes 7953533 | solution.py:61
  183.0 1.4 fusion.47
  185.0 1.7 fusion.51
  186.8 1.4 fusion.47
  188.8 1.7 fusion.51
  190.6 1.4 fusion.47
  192.7 1.7 fusion.51
  194.4 1.4 fusion.47
  195.8 0.6 fusion.49
  196.5 1.7 fusion.51
  198.2 1.4 fusion.47
  200.3 1.7 fusion.51
  202.0 1.4 fusion.47
  204.1 1.7 fusion.51
  205.8 1.4 fusion.47
  207.9 1.7 fusion.51
  209.6 1.4 fusion.47
  211.7 1.7 fusion.51
  213.4 1.4 fusion.47
  215.5 1.7 fusion.51
  217.2 1.4 fusion.47
  219.3 1.7 fusion.51
  221.0 1.4 fusion.47
  223.1 1.7 fusion.51
  224.9 1.4 fusion.47
  226.9 1.7 fusion.51
  228.7 1.4 fusion.47
  230.1 0.6 fusion.49
  230.7 1.7 fusion.51
  232.5 1.4 fusion.47
  233.9 0.6 fusion.49
  234.5 1.7 fusion.51
  236.3 1.4 fusion.47
  238.3 1.7 fusion.51
  240.1 1.4 fusion.47
  242.1 1.7 fusion.51
  244.8 0.8 reduce.2
  245.7 9.8 %all_to_all.33 = bf16[8,2,8192]{2,1,0:T(2,128)(2,1)S(1)} all-to-all(bf16[8,2,8192]{2,1,0:T(2,128)(2,1)S(1)} %reshape.133), channel_id=1, replica_groups=mesh['blk'=8,'uly'=8,'tp'=8] {'uly'}, dimensions={0} | all-to-all | bytes 524288 | tf_op jit(solution)/shard_map/all_to_all | solution.py:104
  255.8 0.9 copy.27
  (94 shorter events, 10.3 us)
Async XLA Ops:
  6.5 92.5 %all-gather.3.cloned.1.call-start = ((), (), s32[]{:S(2)}) async-start(), calls=%async_computation.2 | async-start | bytes 2129920 | tf_op jit(solution)/shard_map/all_gather | solution.py:98
  7.3 175.7 %all-gather.5.cloned.1.call-start = ((), (), s32[]{:S(2)}) async-start(), calls=%async_computation.3 | async-start | bytes 2129920 | tf_op jit(solution)/shard_map/all_gather | solution.py:99
  9.7 16.7 %all-to-all-start = ((bf16[128,8,128]{2,0,1:T(8,128)(2,1)}), bf16[128,8,128]{2,0,1:T(8,128)(2,1)S(1)}, u32[]{:S(2)}, u32[]{:S(2)}) async-start(bf16[128,8,128]{2,0,1:T(8,128)(2,1)} %copy.22), calls=%async_computation | async-start | bytes 524288 | tf_op jit(solution)/shard_map/all_to_all | solution.py:87
Sparse Core Ops, SparseCore 0:
  10.7 88.3 all-gather.2
  102.4 80.5 all-gather.4
where the time goes:
time: 264 us; the launch traced here: 263 us
  waiting for transfers between devices  163 us (62%)
  matrix products  49 us (19%)
  between operations  13.5 us (5%)
  other arithmetic  13.2 us (5%)
  starting transfers between devices  10.2 us (4%)
  blocking collectives  9.79 us (4%)
  local copies, waits for them, and re-layouts  3.84 us (1%)
    all_gather x1, waiting for transfers between devices, local(): lax.all_gather(values, ('blk', 'uly'), axis=0, tiled=True)  83.9 us
    all_gather x1, waiting for transfers between devices, local(): lax.all_gather(keys, ('blk', 'uly'), axis=0, tiled=True)  72.7 us
    dot_general x16, matrix products, attend_block(): jnp.einsum('rhgp,phd->rhgd', weights.astype(jnp.bfloat16), value_block, p...  27.1 us
    dot_general x16, matrix products, attend_block(): jnp.einsum('rhgd,phd->rhgp', query_four, key_block, preferred_element_typ...  21.9 us
    all_to_all x1, starting transfers between devices, local(): lax.all_to_all(queries, 'uly', split_axis=1, concat_axis=0, tiled=True)  10.2 us
    reduce_sum x16, other arithmetic, attend_block(): running_sum = running_sum * rescale + jnp.sum(weights, axis=3)  9.98 us
    all_to_all x1, blocking collectives, local(): lax.all_to_all(head_output, 'uly', split_axis=0, concat_axis=1, tiled=True)  9.79 us
  transfers between devices with their start and end apart: 3, of which 3 were waited for; matrix products, arithmetic and copies ran while one was open for 1% of the time, Pallas kernels for 0%

commit v1 on v0

--- a/solution.py
+++ b/solution.py
@@ -96,7 +96,12 @@
         initial_state(query_four),
         (
             lax.all_gather(keys, ("blk", "uly"), axis=0, tiled=True),
-            lax.all_gather(values, ("blk", "uly"), axis=0, tiled=True),
+            jnp.concatenate(
+                lax.all_to_all(
+                    jnp.stack([values] * lax.axis_size(("blk", "uly"))), ("blk", "uly"), 0, 0
+                ),
+                axis=0,
+            ),
         ),
         jnp.int32(0),
     )

time: 264 us -> 207 us (0.78)
  waiting for transfers between devices: 163 us -> 93.5 us
  blocking collectives: 9.79 us -> 25.6 us
  starting transfers between devices: 10.2 us -> 6.13 us
    all_gather x1 -> x0, waiting for transfers between devices: 83.9 us -> none  [local(): lax.all_gather(values, ('blk', 'uly'), axis=0, tiled=True)]
    all_to_all x1, waiting for transfers between devices: 4.82 us -> 50 us  [local(): lax.all_to_all(jnp.stack([values] * lax.axis_size(('blk', 'uly'))), ('blk...]
    all_gather x1, waiting for transfers between devices: 72.7 us -> 42.8 us  [local(): lax.all_gather(keys, ('blk', 'uly'), axis=0, tiled=True)]
    all_to_all x0 -> x1, blocking collectives: none -> 15.8 us  [local(): lax.all_to_all(queries, 'uly', split_axis=1, concat_axis=0, tiled=True)]
    all_to_all x1, starting transfers between devices: 10.2 us -> 6.09 us  [local(): lax.all_to_all(jnp.stack([values] * lax.axis_size(('blk', 'uly'))), ('blk...]
  transfers between devices with their start and end apart: 3 -> 2, of which waited for: 3 -> 2; matrix products, arithmetic and copies ran while one was open for 1% -> 0% of each run, Pallas kernels for 0% -> 0%
where the time goes in v1:
time: 207 us; the launch traced here: 206 us
  waiting for transfers between devices  93.5 us (45%)
  matrix products  49 us (24%)
  blocking collectives  25.6 us (12%)
  between operations  13.5 us (7%)
  other arithmetic  11.9 us (6%)
  starting transfers between devices  6.13 us (3%)
  local copies, waits for them, and re-layouts  5.73 us (3%)
    all_to_all x1, waiting for transfers between devices, local(): lax.all_to_all(jnp.stack([values] * lax.axis_size(('blk', 'uly'))), ('blk...  50 us
    all_gather x1, waiting for transfers between devices, local(): lax.all_gather(keys, ('blk', 'uly'), axis=0, tiled=True)  42.8 us
    dot_general x16, matrix products, attend_block(): jnp.einsum('rhgp,phd->rhgd', weights.astype(jnp.bfloat16), value_block, p...  27.1 us
    dot_general x16, matrix products, attend_block(): jnp.einsum('rhgd,phd->rhgp', query_four, key_block, preferred_element_typ...  21.8 us
    all_to_all x1, blocking collectives, local(): lax.all_to_all(queries, 'uly', split_axis=1, concat_axis=0, tiled=True)  15.8 us
    reduce_sum x16, other arithmetic, attend_block(): running_sum = running_sum * rescale + jnp.sum(weights, axis=3)  9.98 us
    all_to_all x1, blocking collectives, local(): lax.all_to_all(head_output, 'uly', split_axis=0, concat_axis=1, tiled=True)  9.79 us
    all_to_all x1, starting transfers between devices, local(): lax.all_to_all(jnp.stack([values] * lax.axis_size(('blk', 'uly'))), ('blk...  6.09 us
  transfers between devices with their start and end apart: 2, of which 2 were waited for; matrix products, arithmetic and copies ran while one was open for 0% of the time, Pallas kernels for 0%

profile of v1, /device:TPU:1, one launch (start us, length us, event | category | flops | bytes accessed | tf_op | source)
XLA Modules:
  0.0 206.5 jit_solution(14951483224175524179)
XLA Ops:
  6.5 1.0 copy.22
  7.5 15.8 %all_to_all.38 = bf16[128,8,128]{2,0,1:T(8,128)(2,1)S(1)} all-to-all(bf16[128,8,128]{2,0,1:T(8,128)(2,1)S(1)} %copy.22), channel_id=1, replica_groups=mesh['blk'=8,'uly'=8,'tp'=8] {'uly'}, dimensions={1} | all-to-all | bytes 524288 | tf_op jit(solution)/shard_map/all_to_all | solution.py:87
  23.3 2.6 %stack.2 = bf16[64,128,1,128]{3,1,2,0:T(8,128)(2,1)} broadcast(bf16[128,128]{1,0:T(8,128)(2,1)} %bitcast.99), dimensions={1,3} | broadcast | bytes 2129920 | tf_op jit(solution)/shard_map/stack | solution.py:101
  25.9 6.1 %all-to-all-start.1 = ((bf16[64,128,1,128]{3,1,2,0:T(8,128)(2,1)}), bf16[64,128,1,128]{3,1,2,0:T(8,128)(2,1)}, u32[]{:S(2)}, u32[]{:S(2)}) async-start(bf16[64,128,1,128]{3,1,2,0:T(8,128)(2,1)} %stack.2), calls=%async_computation.1 | async-start | bytes 4194304 | tf_op jit(solution)/shard_map/all_to_all | solution.py:100
  32.1 0.7 all-gather.2.cloned.1.call-update
  33.2 50.0 %all-to-all-done.1 = bf16[64,128,1,128]{3,1,2,0:T(8,128)(2,1)} async-done(((bf16[64,128,1,128]{3,1,2,0:T(8,128)(2,1)}), bf16[64,128,1,128]{3,1,2,0:T(8,128)(2,1)}, u32[]{:S(2)}, u32[]{:S(2)}) %all-to-all-start.1) | async-done | bytes 2097184 | tf_op jit(solution)/shard_map/all_to_all | solution.py:100
  83.2 42.8 %all-gather.2.cloned.1.call-done = bf16[8192,1,128]{2,0,1:T(8,128)(2,1)} async-done(((bf16[128,1,128]{2,0,1:T(8,128)(2,1)}), bf16[8192,1,128]{2,0,1:T(8,128)(2,1)}) %all-gather.2.cloned.1.call-update) | async-done | bytes 2097168 | tf_op jit(solution)/shard_map/all_gather | solution.py:98
  126.0 60.8 %while.15 = (s32[]{:T(128)}, f32[1024,1,1]{0,2,1:T(1,128)S(1)}, f32[1024,1,1]{0,2,1:T(1,128)S(1)}, f32[1024,1,1,128]{0,3,2,1:T(8,128)S(1)}, s32[16,512]{1,0:T(8,...) while((s32[]{:T(128)}, f32[1024,1,1]{0,2,1:T(1,128)S(1)}, ...), condition=%wide.region_5.6_spmd.clone, body=%wide.region_2.5_spmd.clone.sunk | while | flops 277222400 | bytes 7953533 | solution.py:61
  126.0 1.4 fusion.47
  127.4 0.6 fusion.49
  128.1 1.7 fusion.51
  129.8 1.4 fusion.47
  131.2 0.6 fusion.49
  131.9 1.7 fusion.51
  133.6 1.4 fusion.47
  135.0 0.6 fusion.49
  135.7 1.7 fusion.51
  137.4 1.4 fusion.47
  138.8 0.6 fusion.49
  139.5 1.7 fusion.51
  141.2 1.4 fusion.47
  142.6 0.6 fusion.49
  143.3 1.7 fusion.51
  145.0 1.4 fusion.47
  147.1 1.7 fusion.51
  148.8 1.4 fusion.47
  150.9 1.7 fusion.51
  152.6 1.4 fusion.47
  154.7 1.7 fusion.51
  156.4 1.4 fusion.47
  158.5 1.7 fusion.51
  160.2 1.4 fusion.47
  162.3 1.7 fusion.51
  164.0 1.4 fusion.47
  166.1 1.7 fusion.51
  167.8 1.4 fusion.47
  169.9 1.7 fusion.51
  171.6 1.4 fusion.47
  173.7 1.7 fusion.51
  175.4 1.4 fusion.47
  177.5 1.7 fusion.51
  179.2 1.4 fusion.47
  181.3 1.7 fusion.51
  183.0 1.4 fusion.47
  185.1 1.7 fusion.51
  187.7 0.8 reduce.2
  188.6 9.8 %all_to_all.39 = bf16[8,2,8192]{2,1,0:T(2,128)(2,1)S(1)} all-to-all(bf16[8,2,8192]{2,1,0:T(2,128)(2,1)S(1)} %reshape.132), channel_id=1, replica_groups=mesh['blk'=8,'uly'=8,'tp'=8] {'uly'}, dimensions={0} | all-to-all | bytes 524288 | tf_op jit(solution)/shard_map/all_to_all | solution.py:109
  198.7 0.9 copy.27
  (95 shorter events, 9.3 us)
Async XLA Ops:
  25.9 6.9 %copy-start = (s32[16]{0:T(128)S(1)}, s32[16]{0:T(128)}, u32[]{:S(2)}) copy-start(s32[16]{0:T(128)} %param.9) | copy-start | bytes 196
  25.9 57.3 %all-to-all-start.1 = ((bf16[64,128,1,128]{3,1,2,0:T(8,128)(2,1)}), bf16[64,128,1,128]{3,1,2,0:T(8,128)(2,1)}, u32[]{:S(2)}, u32[]{:S(2)}) async-start(bf16[64,128,1,128]{3,1,2,0:T(8,128)(2,1)} %stack.2), calls=%async_computation.1 | async-start | bytes 4194304 | tf_op jit(solution)/shard_map/all_to_all | solution.py:100
  32.0 94.0 %all-gather.2.cloned.1.call-start = ((), (), s32[]{:S(2)}) async-start(), calls=%async_computation.3 | async-start | bytes 2129920 | tf_op jit(solution)/shard_map/all_gather | solution.py:98
Sparse Core Ops, SparseCore 0:
  36.2 89.7 all-gather.1
